TPU v7x, 32 devices: a whole 2x2x4 slice. The times are simulated.
32 devices in a mesh: cls: 4 (over z), vol: 8 (over y, x, core).
Axes of the slice: x: 2, y: 2, z: 4, core: 2. Of those that a mesh axis runs over, the one named last changes fastest.
Arguments:
- images: bfloat16 [256, 256, 2, 256], P(('cls', 'vol')), may hold values from -8 to 8
- projections: bfloat16 [4, 128, 256, 2, 256], P('cls', None, 'vol'), may hold values from -0.049718446 to 0.049718446
- assignment: int32 [256, 1], P(('cls', 'vol')), may hold values from 0 to 3; in each aligned block of 8 rows (0 to 7, 8 to 15, ...) at most 4 rows name the same one
- interp_cells: int32 [128, 4, 256], replicated, may hold values from 0 to 65535, as said below
- interp_weights: float32 [128, 4, 256], replicated, may hold values from 0 to 1, as said below
Outputs:
- class_volume: float32 [4, 256, 256, 256], P('cls', 'vol')
Inputs may be any that keep to these rules, and one draw needn't show every extreme that they name: `assignment`: among the 8 particles of one device (aligned blocks of 8 rows), at most 4 name the same class. `interp_cells`: for each direction and column u the four cells are (x, y), (x + 1, y), (x, y + 1), (x + 1, y + 1) modulo 256, in that order. `interp_weights`: for each direction and column u the four weights are nonnegative and sum to one.
All inputs are finite; a program needn't handle non-finite values.
Results may differ from a plain program's by a relative error of at most 0.0027.
Values may be sent and summed in bfloat16 or wider, within the bound.
No kernel may reach another device: no remote copies, remote signals or barrier semaphores. Data moves between devices by JAX's collectives and lax.ppermute only.
A program may use at most 256 MiB of HBM per device.

v0:
```python
import functools
import math

import jax
import jax.numpy as jnp
import numpy as np
from jax import lax
from jax.experimental import pallas as pl
from jax.experimental.pallas import tpu as pltpu
from jax.sharding import PartitionSpec as P

F32 = jnp.float32
BF16 = jnp.bfloat16
LANES = 128
HALF = 64
CHUNK = 128
PAD = 8
UNROLL = 16
STEP = 16
VMEM = pltpu.VMEM


def split_table(table):
    high = table.astype(jnp.bfloat16)
    low = (table - high.astype(np.float64)).astype(jnp.bfloat16)
    return high, low


def plane_pairs(grid, slabs):
    slab = grid // slabs
    half = slab // 2
    pairs = []
    for w in range(slabs):
        for i in range(half):
            if w < slabs // 2:
                first = slab * w + 1 + i
            else:
                first = slab * w + half - 1 - i
            if 2 * first == grid:
                pairs.append((0, first))
            else:
                pairs.append((first, grid - first))
    return np.array(pairs).reshape(slabs, half, 2)


def tables(grid, slabs):
    half = grid // 2
    scale = 1.0 / math.sqrt(grid)
    index = np.arange(grid)
    angle = 2.0 * np.pi / grid
    phase = (index[:, None] * np.arange(half)[None, :]) % grid
    cosine = np.cos(phase * angle)
    sine = np.sin(phase * angle)
    sine[:, 0] = np.cos(((index * half) % grid) * angle)
    table_y = np.concatenate([cosine, sine], axis=1) * scale
    rows = half + 8
    phase = (np.arange(rows)[:, None] * index[None, :]) % grid
    live = (np.arange(rows) <= half)[:, None]
    table_x = np.concatenate([np.cos(phase * angle) * live, np.sin(phase * angle) * live], axis=0) * scale
    pairs = plane_pairs(grid, slabs).reshape(-1, 2)
    single = (2 * pairs[:, 1] == grid)[:, None]
    z = np.where(single[:, 0], pairs[:, 1], pairs[:, 0])
    phase = (z[:, None] * index[None, :]) % grid
    for_sum = np.where(single, 1.0, np.cos(phase * angle))
    for_difference = np.where(single, np.cos(phase * angle), -np.sin(phase * angle))
    table_z = np.stack([for_sum, for_difference], axis=1).reshape(grid, grid) * scale
    order = np.concatenate([np.arange(half), [half], np.arange(grid - 1, half, -1)])
    restore = (order[None, :] == index[:, None]).astype(jnp.bfloat16)
    parts = max(1, grid // slabs // STEP)
    table_z = table_z.reshape(slabs, parts, -1, grid).transpose(1, 0, 2, 3).reshape(grid, grid)
    high, low = split_table(table_y)
    table_y = np.concatenate([high, high, low], axis=0)
    high, low = split_table(table_x)
    table_x = np.concatenate([high, high, low], axis=1)
    table_z = np.concatenate(split_table(table_z), axis=0)
    return table_y, table_x, table_z, restore


def lane_order(grid, slabs):
    rows = plane_pairs(grid, slabs).transpose(0, 2, 1).reshape(-1)
    source = (2 * rows[:, None] + np.arange(2)[None, :]).reshape(-1)
    return (np.arange(2 * grid)[:, None] == source[None, :]).astype(jnp.bfloat16)


def dot(a, b):
    return jnp.dot(a, b, preferred_element_type=F32)


def dot_t(a, b):
    return lax.dot_general(a, b, (((1,), (1,)), ((), ())), preferred_element_type=F32)


def two_terms(value):
    high = value.astype(BF16)
    low = (value - high.astype(F32)).astype(BF16)
    return high, low


def route_kernel(cap, slabs, width, classes_ref, images_ref, eye_ref, order_ref, out_ref, lines):
    count, _, _, grid = images_ref.shape
    halves = LANES // width
    piece = grid // halves
    lane = lax.broadcasted_iota(jnp.int32, (piece, LANES), 1)
    lines[...] = jnp.zeros_like(lines)

    def place(p, carry):
        own = classes_ref[p, 0]
        rank = 0
        for q in range(count):
            rank = rank + jnp.where((classes_ref[q, 0] == own) & (q < p), 1, 0)
        image = images_ref[p].reshape(-1, grid)
        turned = dot(dot_t(eye_ref[...], image).astype(BF16), order_ref[...])
        for w in range(slabs):
            tile = w * width // LANES * LANES
            block = jnp.zeros((piece, LANES), F32)
            for h in range(halves):
                part = turned[h * piece : (h + 1) * piece, tile : tile + LANES]
                shift = (h * width - (w * width - tile)) % LANES
                part = part if shift == 0 else pltpu.roll(part, shift, 1)
                block = jnp.where((lane >= h * width) & (lane < (h + 1) * width), part, block)
            lines[own * slabs + w, pl.ds(rank, piece, stride=cap), :] = block
        return carry

    lax.fori_loop(0, count, place, 0, unroll=2)
    out_ref[...] = lines[...].astype(BF16).reshape(out_ref.shape)


def route_call(images, assignment, eye, order, class_count, slabs, width, cap):
    count, grid = images.shape[0], images.shape[1]
    rows = grid // (LANES // width) * cap
    vmem = pl.BlockSpec(memory_space=VMEM)
    return pl.pallas_call(
        functools.partial(route_kernel, cap, slabs, width),
        out_shape=jax.ShapeDtypeStruct((class_count * slabs, rows // 16, 16, LANES), BF16),
        in_specs=[pl.BlockSpec(memory_space=pltpu.SMEM)] + [vmem] * 3,
        out_specs=vmem,
        scratch_shapes=[VMEM((class_count * slabs, rows, LANES), F32)],
        compiler_params=pltpu.CompilerParams(vmem_limit_bytes=48 * 2**20),
        name="route",
    )(assignment, images, eye, order)


def score_kernel(cap, dirs, unit, first_ref, second_ref, kept_ref, joined_ref, out_ref, sums):
    sources, groups, rows16, _ = first_ref.shape
    rows = sources * rows16
    steps = rows16 // cap
    lane = lax.broadcasted_iota(jnp.int32, (steps * dirs, LANES), 1)
    even = (lane & unit) == 0

    @pl.when(pl.program_id(0) == 0)
    def _():
        sums[...] = jnp.zeros_like(sums)

    for g in range(groups):
        kept = kept_ref[g].astype(F32)
        joined = joined_ref[g].astype(F32)
        refs = [
            jnp.where(even, kept, pltpu.roll(joined, unit, 1)).astype(BF16),
            jnp.where(even, pltpu.roll(kept, LANES - unit, 1), joined).astype(BF16),
        ]
        blocks = [ref[:, g].reshape(rows, LANES) for ref in (first_ref, second_ref)]
        sums[...] += dot_t(jnp.concatenate(refs, axis=1), jnp.concatenate(blocks, axis=1))

    @pl.when(pl.program_id(0) == pl.num_programs(0) - 1)
    def _():
        column = lax.broadcasted_iota(jnp.int32, (dirs, rows), 1)
        part = (column & (rows16 - 1)) // cap
        kept = jnp.zeros((dirs, rows), F32)
        for j in range(steps):
            kept = kept + jnp.where(part == j, sums[j * dirs : (j + 1) * dirs, :], 0.0)
        slots = sources * cap
        row_id = lax.broadcasted_iota(jnp.int32, (rows, slots), 0)
        slot_id = lax.broadcasted_iota(jnp.int32, (rows, slots), 1)
        gather = (row_id // rows16 * cap + row_id % cap) == slot_id
        value = jnp.dot(
            kept, gather.astype(F32), preferred_element_type=F32, precision=lax.Precision.HIGHEST
        )
        for copy in range(out_ref.shape[0]):
            out_ref[copy] = value


def scores_call(images, kept, joined, cap, dirs, unit, slabs):
    sources, groups, rows16, _ = images.shape
    joint = kept.shape[1]
    span = min(4, groups // 2)
    turns = groups // 2 // span
    return pl.pallas_call(
        functools.partial(score_kernel, cap, dirs, unit),
        grid=(turns,),
        out_shape=jax.ShapeDtypeStruct((slabs, dirs, sources * cap), F32),
        in_specs=[
            pl.BlockSpec((sources, span, rows16, LANES), lambda i: (0, i, 0, 0)),
            pl.BlockSpec((sources, span, rows16, LANES), lambda i: (0, i + turns, 0, 0)),
            pl.BlockSpec((span, joint, LANES), lambda i: (i, 0, 0)),
            pl.BlockSpec((span, joint, LANES), lambda i: (i, 0, 0)),
        ],
        out_specs=pl.BlockSpec((slabs, dirs, sources * cap), lambda i: (0, 0, 0)),
        scratch_shapes=[VMEM((joint, sources * rows16), F32)],
        compiler_params=pltpu.CompilerParams(vmem_limit_bytes=48 * 2**20),
        name="scores",
    )(images, images, kept, joined)


def scatter_kernel(
    cap,
    width,
    grid,
    slabs,
    single_ref,
    first_ref,
    point_ref,
    parts_ref,
    images_hbm,
    weights_hbm,
    y_ref,
    x_ref,
    sent_ref,
    *refs,
):
    rest = width > STEP * 2
    rest_hbm = refs[0] if rest else None
    plane, values, sums, spread, lines, images_ref, weights_ref, image_sem, weight_sem, rest_sem, *buffers = refs[rest:]
    sources, groups, rows16, _ = images_ref.shape
    pieces = weight_sem.shape[0]
    images_copy = pltpu.make_async_copy(images_hbm, images_ref, image_sem)
    images_copy.start()
    weight_copies = []
    for i in range(pieces):
        part = pl.ds(i * (groups // pieces), groups // pieces)
        weight_copies.append(pltpu.make_async_copy(weights_hbm.at[part], weights_ref.at[part], weight_sem.at[i]))
        weight_copies[i].start()
    rows = sources * rows16
    steps = rows16 // cap
    dirs, slots = parts_ref.shape[1:]
    joined = steps * dirs
    halves = LANES // width

    total = parts_ref[0]
    for i in range(1, parts_ref.shape[0]):
        total = total + parts_ref[i]
    expo = jnp.exp(total - jnp.max(total, axis=0, keepdims=True))
    posterior = (expo / jnp.sum(expo, axis=0, keepdims=True)).astype(BF16)
    slot_id = lax.broadcasted_iota(jnp.int32, (slots, rows), 0)
    row_id = lax.broadcasted_iota(jnp.int32, (slots, rows), 1)
    repeat = ((row_id // rows16 * cap + row_id % cap) == slot_id).astype(F32).astype(BF16)
    wide = dot(posterior, repeat)
    part = (lax.broadcasted_iota(jnp.int32, (dirs, rows), 1) & (rows16 - 1)) // cap
    for j in range(steps):
        spread[j * dirs : (j + 1) * dirs, :] = jnp.where(part == j, wide, 0.0).astype(BF16)

    lane_j = lax.broadcasted_iota(jnp.int32, (joined, LANES), 1)

    def average(m, carry):
        blocks = [images_ref[:, pl.ds(2 * m + i, 1), :, :].reshape(rows, LANES) for i in range(2)]
        means = dot(spread[...], jnp.concatenate(blocks, axis=1))
        for i in range(2):
            g = 2 * m + i
            mean = means[:, i * LANES : (i + 1) * LANES]
            weight = weights_ref[g]
            for h in range(halves):
                shifted = mean if h == 0 else pltpu.roll(mean, LANES - h * width, 1)
                behind = pltpu.roll(weight, HALF - 8 * h, 1)
                start = pl.multiple_of((h * groups + g) * joined, joined)
                values[pl.ds(start, joined), :] = jnp.where(lane_j < HALF, shifted, behind)
        return carry

    images_copy.wait()
    for i in range(pieces):
        weight_copies[i].wait()
        begin = groups // pieces // 2
        lax.fori_loop(i * begin, (i + 1) * begin, average, 0)

    for buffer in buffers:
        buffer[...] = jnp.zeros_like(buffer)
    sums[...] = jnp.zeros_like(sums)

    place = lax.broadcasted_iota(jnp.int32, (CHUNK, LANES), 0)
    lane = lax.broadcasted_iota(jnp.int32, (CHUNK, grid), 1)
    at_y = lane.astype(F32).astype(BF16)
    at_next = ((lane + (grid - 1)) & (grid - 1)).astype(F32).astype(BF16)
    line_8 = lax.broadcasted_iota(jnp.int32, (8, LANES), 0)
    one = jnp.ones((CHUNK, grid), BF16)
    none = jnp.zeros((CHUNK, grid), BF16)

    lane_1 = lax.broadcasted_iota(jnp.int32, (1, CHUNK), 1)
    points = values.shape[0]

    def fetch(start, buffer):
        for i in range(0, CHUNK, 8):
            block = jnp.broadcast_to(values[pl.ds(point_ref[start + i], 1), :], (8, LANES))
            for j in range(1, 8):
                line = jnp.broadcast_to(values[pl.ds(point_ref[start + i + j], 1), :], (8, LANES))
                block = jnp.where(line_8 == j, line, block)
            buffer[i : i + 8, :] = block

    def put(row, value):
        x = (row + (grid - 1)) & (grid - 1)
        for side in range(grid // LANES):
            plane[side, x, :width, :] = value[:, side * LANES : (side + 1) * LANES]

    def combined(mean):
        a, b = mean[: width // 2], mean[width // 2 :]
        total, gap = a + b, a - b
        tile = width // 2 - 8
        special = (single_ref[0] == 1) & (line_8 >= 6)
        moved = jnp.where(line_8 == 6, -pltpu.roll(b[tile:], 7, 0), pltpu.roll(b[tile:], 1, 0))
        total = [total[:tile], jnp.where(special, a[tile:], total[tile:])]
        gap = [gap[:tile], jnp.where(special, moved, gap[tile:])]
        return jnp.concatenate([part for part in total + gap if part.shape[0]], axis=0)

    def following(start, row):
        second, third = first_ref[row + 1], first_ref[row + 2]
        end = jnp.minimum(start + CHUNK, third)
        moved = row + jnp.where(end >= second, 1, 0) + jnp.where(end >= third, 1, 0)
        return end, jnp.minimum(moved, grid - 1), end - start, jnp.clip(second - start, 0, end - start)

    def work(row, before, size, size_0, buffer):
        data = buffer[...]
        y = jnp.broadcast_to(data[:, HALF + 4 : HALF + 5], (CHUNK, LANES))
        y = jnp.where(place < size, y, -1.0).astype(BF16)
        y = jnp.concatenate([y] * (grid // LANES), axis=1)
        hot = jnp.concatenate([jnp.where(at_y == y, one, none), jnp.where(at_next == y, one, none)], axis=0)
        turned = data.T
        mean = combined(turned[:width])
        weight = [turned[HALF + j : HALF + j + 1] for j in range(4)]
        here = [jnp.where(lane_1 < size_0, w, 0.0) for w in weight]
        there = [w - h for w, h in zip(weight, here)]
        by_row = (
            (here[0], here[2]),
            (here[1] + there[0], here[3] + there[2]),
            (there[1], there[3]),
        )
        operand = jnp.concatenate(
            [
                jnp.concatenate([mean * jnp.broadcast_to(w, (width, CHUNK)) for w in pair], axis=1)
                for pair in by_row
            ],
            axis=0,
        )
        result = dot(operand.astype(BF16), hot)
        old = [sums[i * width : (i + 1) * width] for i in range(3)]
        put(jnp.minimum(before + 1, grid - 1), old[1])
        put(before, old[0])
        stay, by_one = row == before, row == before + 1
        kept = (
            jnp.where(stay, old[0], jnp.where(by_one, old[1], old[2])),
            jnp.where(stay, old[1], jnp.where(by_one, old[2], 0.0)),
            jnp.where(stay, old[2], 0.0),
        )
        for i in range(3):
            sums[i * width : (i + 1) * width] = result[i * width : (i + 1) * width] + kept[i]

    fetch(0, buffers[0])

    def several(state):
        start, row, before = state
        for i in range(UNROLL):
            end, moved, size, size_0 = following(start, row)
            fetch(end, buffers[(i + 1) % UNROLL])
            work(row, before, size, size_0, buffers[i])
            start, row, before = end, moved, row
        return start, row, before

    zero = jnp.int32(0)
    lax.while_loop(lambda state: (state[0] < points) | (state[2] < grid - 1), several, (zero, zero, zero))
    put(grid - 1, sums[:width])
    for side in range(grid // LANES):
        cut = slice(side * LANES, (side + 1) * LANES)
        plane[side, grid - 1, :width, :] = plane[side, grid - 1, :width, :] + sums[width : 2 * width, cut]

    step = min(STEP, width // 2)
    copies = []
    if rest:
        for part in range(grid // LANES):
            for side in range(2):
                source = plane.at[part, :, pl.ds(side * (width // 2) + step, width // 2 - step)]
                copies.append(pltpu.make_async_copy(source, rest_hbm.at[part, side], rest_sem.at[2 * part + side]))
                copies[-1].start()

    pitch = width + PAD
    flat = plane.reshape(grid // LANES, grid * pitch, LANES)

    def load(part, side, value):
        return flat[part, pl.ds(side * (width // 2) + value, grid, stride=pitch), :]

    transform_pairs(slabs, grid, step // 2, load, y_ref, x_ref, sent_ref, lines)
    for copy in copies:
        copy.wait()


def scatter_call(single, plan, parts, images, weights, table_y, table_x, cap, width, grid, slabs):
    sources, groups, rows16, _ = images.shape
    dirs = parts.shape[1]
    points = dirs * grid
    smem = pl.BlockSpec(memory_space=pltpu.SMEM)
    vmem = pl.BlockSpec(memory_space=VMEM)
    hbm = pl.BlockSpec(memory_space=pl.ANY)
    step = min(STEP, width // 2)
    other = width // 2 - step
    sides = grid // LANES
    pieces = 4
    shapes = [jax.ShapeDtypeStruct((slabs, grid // slabs, step, grid), BF16)]
    if other:
        shapes.append(jax.ShapeDtypeStruct((sides, 2, grid, other, LANES), F32))
    result = pl.pallas_call(
        functools.partial(scatter_kernel, cap, width, grid, slabs),
        out_shape=shapes,
        in_specs=[smem] * 3 + [vmem, hbm, hbm, vmem, vmem],
        out_specs=[vmem, hbm][: len(shapes)],
        scratch_shapes=[
            VMEM((sides, grid, width + PAD, LANES), F32),
            VMEM((points, LANES), F32),
            VMEM((3 * width, grid), F32),
            VMEM((weights.shape[1], sources * rows16), BF16),
            VMEM((sides, grid * step, LANES), F32),
            VMEM(images.shape, BF16),
            VMEM(weights.shape, F32),
            pltpu.SemaphoreType.DMA,
            pltpu.SemaphoreType.DMA((pieces,)),
            pltpu.SemaphoreType.DMA((2 * sides,)),
        ]
        + [VMEM((CHUNK, LANES), F32)] * UNROLL,
        compiler_params=pltpu.CompilerParams(vmem_limit_bytes=61 * 2**20),
        name="scatter",
    )(single, *plan, parts, images, weights, table_y, table_x)
    if not other:
        return result[0], None
    return result[0], result[1].reshape(sides, 2, grid * other, LANES)


def transform_pairs(slabs, grid, pairs, load, y_ref, x_ref, out_ref, lines):
    half = grid // 2
    rows = half + 8
    slab = grid // slabs
    count = 2 * pairs
    lane = lax.broadcasted_iota(jnp.int32, (grid, half), 1)

    def transformed(real, imag):
        cos_r, sin_r = real[:, :half], real[:, half:]
        cos_i, sin_i = imag[:, :half], imag[:, half:]
        zero_r = jnp.where(lane == 0, 0.0, sin_r)
        zero_i = jnp.where(lane == 0, 0.0, sin_i)
        real = jnp.concatenate([cos_r - zero_i, jnp.where(lane == 0, sin_r, cos_r + sin_i)], axis=1)
        imag = jnp.concatenate([cos_i + zero_r, jnp.where(lane == 0, sin_i, cos_i - sin_r)], axis=1)
        return real, imag

    def along_x(table, operand):
        high, low = two_terms(operand)
        return dot(x_ref[table * rows : (table + 1) * rows], jnp.concatenate([high, low, high], axis=0))

    def one(i, carry):
        planes = [
            jnp.concatenate([load(part, side, 2 * i + r) for part in range(grid // LANES)], axis=1)
            for side in range(2)
            for r in range(2)
        ]
        both = []
        for value in planes:
            high, low = two_terms(value)
            both.append(dot(jnp.concatenate([high, low, high], axis=1), y_ref[...]))
        sum_r, sum_i = transformed(both[0], both[1])
        dif_r, dif_i = transformed(both[2], both[3])
        cosine = along_x(0, jnp.concatenate([sum_r, dif_i], axis=1))
        sine = along_x(1, jnp.concatenate([sum_i, dif_r], axis=1))
        fields = (
            (cosine[:, :grid] - sine[:, :grid], cosine[:, :grid] + sine[:, :grid]),
            (cosine[:, grid:] + sine[:, grid:], cosine[:, grid:] - sine[:, grid:]),
        )
        for c in range(2):
            plus, minus = fields[c]
            for part in range(grid // LANES):
                cut = slice(part * LANES, (part + 1) * LANES)
                place = 2 * i + c
                lines[part, pl.ds(place, half, stride=count), :] = plus[:half, cut]
                lines[part, pl.ds(half * count + place, half, stride=count), :] = minus[1 : half + 1, cut]
        return carry

    lax.fori_loop(0, pairs, one, 0, unroll=2)
    for d in range(slabs):
        if d < slabs // 2:
            start = slab * d
        else:
            start = half + grid - slab * d - slab
        size = slab * count
        for part in range(grid // LANES):
            block = lines[part, start * count : start * count + size, :]
            out_ref[d, :, :, part * LANES : (part + 1) * LANES] = block.astype(BF16).reshape(slab, count, LANES)


def plane_kernel(slabs, grid, data_ref, y_ref, x_ref, out_ref, lines):
    pitch = data_ref.shape[2] // grid
    pairs = pitch // 2

    def load(part, side, value):
        return data_ref[part, side, pl.ds(value, grid, stride=pitch), :]

    transform_pairs(slabs, grid, pairs, load, y_ref, x_ref, out_ref, lines)


def planes_call(data, table_y, table_x, slabs, grid):
    step = data.shape[2] // grid
    slab = grid // slabs
    vmem = pl.BlockSpec(memory_space=VMEM)
    return pl.pallas_call(
        functools.partial(plane_kernel, slabs, grid),
        in_specs=[vmem] * 3,
        out_specs=vmem,
        scratch_shapes=[VMEM((data.shape[0], grid * step, LANES), F32)],
        out_shape=jax.ShapeDtypeStruct((slabs, slab, step, grid), BF16),
        compiler_params=pltpu.CompilerParams(vmem_limit_bytes=56 * 2**20),
        name="planes",
    )(data, table_y, table_x)


def volume_kernel(flip_ref, restore_ref, z_ref, *refs):
    out_ref = refs[-1]
    slabs, span, width, grid = refs[0].shape
    turned = []
    for i in range(span):
        block = jnp.concatenate([ref[:, i].reshape(slabs * width, grid) for ref in refs[:-1]], axis=0)
        turned.append(dot_t(restore_ref[...], block).astype(BF16))
    turned = jnp.concatenate(turned, axis=0)
    value = dot(jnp.concatenate([turned, turned], axis=1), z_ref[...])
    for i in range(span):
        out_ref[jnp.where(flip_ref[0] == 1, span - 1 - i, i)] = value[i * grid : (i + 1) * grid]


def volume_call(flip, parts, restore, table_z):
    slabs, slab, width, grid = parts[0].shape
    span = 4
    steps = slab // span
    fixed = lambda i, flip_ref: (0, 0)
    return pl.pallas_call(
        volume_kernel,
        grid_spec=pltpu.PrefetchScalarGridSpec(
            num_scalar_prefetch=1,
            grid=(steps,),
            in_specs=[pl.BlockSpec(restore.shape, fixed), pl.BlockSpec(table_z.shape, fixed)]
            + [pl.BlockSpec((slabs, span, width, grid), lambda i, flip_ref: (0, i, 0, 0))] * len(parts),
            out_specs=pl.BlockSpec(
                (span, grid, grid), lambda i, flip_ref: (jnp.where(flip_ref[0] == 1, steps - 1 - i, i), 0, 0)
            ),
        ),
        out_shape=jax.ShapeDtypeStruct((slab, grid, grid), F32),
        compiler_params=pltpu.CompilerParams(vmem_limit_bytes=48 * 2**20),
        name="volume",
    )(flip, restore, table_z, *parts)


def sorted_points(interp_cells, grid):
    dirs = interp_cells.shape[0]
    points = dirs * grid
    base = interp_cells[:, 0, :].T.reshape(-1)
    row = (base // grid + 1) & (grid - 1)
    key = row * points + jnp.arange(points, dtype=jnp.int32)
    key = lax.sort(key, is_stable=False)
    rows = jnp.arange(grid + 3, dtype=jnp.int32)
    first = jnp.sum((row[None, :] < rows[:, None]).astype(jnp.int32), axis=1)
    point = jnp.concatenate([key & (points - 1), jnp.zeros((CHUNK,), jnp.int32)])
    return first, point


def arrange_kernel(rows_ref, other_ref, eye_ref, order_ref, extra_ref, kept_ref, sent_ref, *lines):
    dirs, count, _, grid = rows_ref.shape
    blocks = LANES // count
    length = grid // blocks
    span = extra_ref.shape[0]
    each = span * blocks
    number = lax.broadcasted_iota(jnp.int32, (length, LANES), 1) // count

    def step(m, carry):
        other = other_ref[pl.ds(pl.multiple_of(2 * each * m, 2 * each), 2 * each), :]
        other = dot_t(eye_ref[...], other).astype(BF16)
        for group in range(span):
            k = each * m + blocks * group
            block = rows_ref[pl.ds(k, blocks)].reshape(2 * LANES, grid)
            turned = dot_t(eye_ref[...], block).astype(BF16)
            turned = dot(turned, order_ref[...]) + dot(other, extra_ref[group])
            for side in range(2):
                tile = [turned[q * length : (q + 1) * length, side * LANES : (side + 1) * LANES] for q in range(blocks)]
                bit = 1
                while bit < blocks:
                    low = (number & bit) == 0
                    swapped = list(tile)
                    for q in range(blocks):
                        if q & bit == 0:
                            swapped[q] = jnp.where(low, tile[q], pltpu.roll(tile[q + bit], bit * count, 1))
                            swapped[q + bit] = jnp.where(low, pltpu.roll(tile[q], LANES - bit * count, 1), tile[q + bit])
                    tile = swapped
                    bit *= 2
                for i in range(blocks):
                    lines[side][pl.ds(k + i, length, stride=dirs + PAD), :] = tile[i]
        return carry

    lax.fori_loop(0, dirs // each, step, 0)
    for side, out_ref in enumerate((kept_ref, sent_ref)):
        steps = out_ref.shape[1] // dirs
        for u in range(length):
            block = lines[side][u * (dirs + PAD) : u * (dirs + PAD) + dirs, :].astype(BF16)
            out_ref[u // steps, u % steps * dirs : (u % steps + 1) * dirs, :] = block


def arrange_call(rows, other, eye, order, extra, steps):
    dirs, count, _, grid = rows.shape
    length = grid // (LANES // count)
    vmem = pl.BlockSpec(memory_space=VMEM)
    shape = jax.ShapeDtypeStruct((length // steps, steps * dirs, LANES), BF16)
    return pl.pallas_call(
        arrange_kernel,
        out_shape=(shape, shape),
        in_specs=[vmem] * 5,
        out_specs=(vmem, vmem),
        scratch_shapes=[VMEM((length * (dirs + PAD), LANES), F32)] * 2,
        compiler_params=pltpu.CompilerParams(vmem_limit_bytes=48 * 2**20),
        name="arrange",
    )(rows, other, eye, order, extra)


def row_orders(slab):
    half = slab // 2
    blocks = LANES // slab
    span = max(1, 8 // blocks)
    down = list(range(half - 1, -1, -1))
    upper = list(range(slab - 1, half - 1, -1))
    orders, extras = [], []
    for kept, sent in (
        (list(range(1, half + 1)), list(range(half + 1, slab)) + [None]),
        (down[:-1] + [None], upper),
        (down, upper),
    ):
        order = np.zeros((2 * LANES, 2 * LANES))
        extra = np.zeros((span, 2 * span * blocks, 2 * LANES))
        for side, rows in enumerate((kept, sent)):
            for k in range(blocks):
                for i, row in enumerate(rows):
                    for r in range(2):
                        lane = side * LANES + k * slab + 2 * i + r
                        if row is not None:
                            order[(k * slab + row) * 2 + r, lane] = 1.0
                        else:
                            for group in range(span):
                                extra[group, (group * blocks + k) * 2 + r, lane] = 1.0
        orders.append(order.astype(jnp.bfloat16))
        extras.append(extra.astype(jnp.bfloat16))
    return np.stack(orders), np.stack(extras)


def paired_rows(rows, eye, slabs, steps):
    own = lax.axis_index("vol")
    dirs, slab, _, grid = rows.shape
    first = [(0, slabs // 2)] + [(i, i - 1) for i in range(1, slabs // 2 + 1)]
    other = lax.ppermute(rows[:, 0], "vol", first).reshape(2 * dirs, grid)
    kind = jnp.where(own < slabs // 2, 0, jnp.where(own == slabs // 2, 1, 2))
    order, extra = (lax.dynamic_index_in_dim(jnp.asarray(t), kind, 0, keepdims=False) for t in row_orders(slab))
    kept, sent = arrange_call(rows, other, eye, order, extra, steps)
    arrived = lax.ppermute(sent, "vol", [(i, slabs - 1 - i) for i in range(slabs)])
    return kept, arrived


def shards(images, projections, assignment, interp_cells, interp_weights):
    class_count = lax.axis_size("cls")
    slab_count = lax.axis_size("vol")
    local_count, grid = images.shape[0], images.shape[1]
    dirs = projections.shape[1]
    slab = grid // slab_count
    width = 2 * slab
    halves = LANES // width
    capacity = 2 * local_count // class_count
    steps = 16 // capacity
    groups = grid // (halves * steps)

    eye = jnp.asarray(np.eye(grid), BF16)
    order = jnp.asarray(lane_order(grid, slab_count))
    outgoing = route_call(images, assignment, eye, order, class_count, slab_count, width, capacity)
    outgoing, projections = lax.optimization_barrier((outgoing, projections))
    arrived = lax.all_to_all(outgoing, ("cls", "vol"), split_axis=0, concat_axis=0, tiled=True)

    kept, joined = paired_rows(projections[0], eye, slab_count, steps)
    corner_y = (interp_cells[:, 0:1, :] & (grid - 1)).astype(F32)
    weights = jnp.concatenate([interp_weights, corner_y, jnp.zeros((dirs, 3, grid), F32)], axis=1)
    weights = weights.reshape(dirs, 8, halves, groups, steps)
    weights = jnp.transpose(weights, (3, 4, 0, 2, 1)).reshape(groups, steps * dirs, 8 * halves)
    weights = jnp.pad(weights, ((0, 0), (0, 0), (0, LANES - 8 * halves)))
    plan = sorted_points(interp_cells, grid)
    table_y, table_x, table_z, restore = tables(grid, slab_count)

    arrived, kept, joined, weights, plan = lax.optimization_barrier((arrived, kept, joined, weights, plan))
    partial_value = scores_call(arrived, kept, joined, capacity, dirs, slab, slab_count)
    parts = lax.all_to_all(partial_value, "vol", split_axis=0, concat_axis=0, tiled=True)
    own = lax.axis_index("vol")
    single = (own == slab_count // 2).astype(jnp.int32).reshape(1)
    flip = (own >= slab_count // 2).astype(jnp.int32).reshape(1)
    sent, plane = scatter_call(
        single, plan, parts, arrived, weights, table_y, table_x, capacity, width, grid, slab_count
    )
    received = [lax.all_to_all(sent, "vol", split_axis=0, concat_axis=0, tiled=True)]
    if plane is not None:
        sent = planes_call(plane, table_y, table_x, slab_count, grid)
        received.append(lax.all_to_all(sent, "vol", split_axis=0, concat_axis=0, tiled=True))
    return volume_call(flip, received, restore, table_z)[None]


def solution(mesh):
    in_specs = (
        P(("cls", "vol"), None, None, None),
        P("cls", None, "vol", None, None),
        P(("cls", "vol"), None),
        P(),
        P(),
    )
    out_specs = P("cls", "vol", None, None)
    return jax.shard_map(shards, mesh=mesh, in_specs=in_specs, out_specs=out_specs, check_vma=False)
```

profile of v0, /device:TPU:0, one launch (start us, length us, event | category | flops | bytes accessed | tf_op | source)
XLA Modules:
  0.0 283.8 jit_solution(4614187251237770373)
XLA Ops:
  0.0 0.7 copy.23.classes_ref
  0.7 0.0 copy-start
  0.7 1.6 copy-done
  2.3 0.0 copy-start.1
  2.3 1.0 copy-done.1
  3.4 0.0 copy-start.2
  3.4 0.9 copy-done.2
  4.3 7.0 %route.1 = bf16[32,32,16,128]{3,2,1,0:T(8,128)(2,1)} custom-call(s32[8,1]{1,0:T(8,128)S(1)} %copy.23.classes_ref, bf16[8,256,2,256]{3,2,1,0:T(2,128)(2,1)S(1)} %copy-done, bf16[256,256]{1,0:T(8,128)(2,1)S(1)} %copy-done.2, bf16[512,512]{1,0:T(8,128)(2,1)S(1)} %copy-done.1), custom_call_target="tpu_custom_call" | custom-call | tf_op jit(solution)/shard_map/route/pallas_call | solution.py:132
  11.3 7.4 %all-to-all-start = ((bf16[32,32,16,128]{3,2,1,0:T(8,128)(2,1)}), bf16[32,32,16,128]{3,2,1,0:T(8,128)(2,1)}, u32[]{:S(2)}, u32[]{:S(2)}) async-start(bf16[32,32,16,128]{3,2,1,0:T(8,128)(2,1)} %route.1), calls=%async_computation | async-start | bytes 8388608 | tf_op jit(solution)/shard_map/all_to_all | solution.py:676
  18.8 1.0 slice_bitcast_fusion
  19.8 3.6 %collective-permute-start = (bf16[128,2,256]{2,1,0:T(2,128)(2,1)S(1)}, bf16[128,2,256]{2,1,0:T(2,128)(2,1)S(1)}, u32[]{:S(2)}, u32[]{:S(2)}) collective-permute-start(bf16[128,2,256]{2,1,0:T(2,128)(2,1)S(1)} %slice_bitcast_fusion), channel_id=1, source_target_pairs={{0,4},{1,0},{2,1},{3,2},{4,3},{8,12},{9,8},{10,9},{11,10},{12,11},... | collective-permute-start | bytes 393224 | tf_op jit(solution)/shard_map/ppermute | solution.py:652
  23.4 0.0 slice-done
  23.4 0.1 copy.31
  23.5 0.0 copy-done.7
  23.5 0.3 copy.25
  23.8 0.1 pad.8.clone
  23.9 0.1 and_convert_fusion
  24.0 0.2 maximum_maximum_fusion
  24.2 0.7 dynamic-slice_bitcast_fusion.1.extra_ref
  24.9 0.3 copy.26
  25.3 0.4 reshape.61
  25.7 4.6 %copy.27 = f32[32,512,16]{2,1,0:T(8,128)} copy(f32[32,512,16]{1,2,0:T(8,128)S(1)} %reshape.61) | data formatting | bytes 2097152 | tf_op jit(solution)/shard_map/reshape | solution.py:682
  30.3 7.6 %pad.5.weights_hbm = f32[32,512,128]{2,1,0:T(8,128)} pad(f32[32,512,16]{2,1,0:T(8,128)} %copy.27, f32[]{:T(128)} %constant.57.clone.1), padding=0_0x0_0x0_112 | pad | bytes 9437188 | tf_op jit(solution)/shard_map/jit(_pad)/pad | solution.py:683
  37.9 0.9 dynamic-slice_bitcast_fusion.order_ref
  38.8 3.9 %collective-permute-done = bf16[128,2,256]{2,1,0:T(2,128)(2,1)S(1)} collective-permute-done((bf16[128,2,256]{2,1,0:T(2,128)(2,1)S(1)}, bf16[128,2,256]{2,1,0:T(2,128)(2,1)S(1)}, u32[]{:S(2)}, u32[]{:S(2)}) %collective-permute-start) | collective-permute-done | bytes 131104 | tf_op jit(solution)/shard_map/ppermute | solution.py:652
  42.7 0.1 reshape.59.other_ref
  42.8 0.0 copy-done.3
  42.8 14.8 %arrange.1 = (bf16[16,512,128]{2,1,0:T(8,128)(2,1)S(1)}, bf16[16,512,128]{2,1,0:T(8,128)(2,1)}) custom-call(bf16[128,32,2,256]{3,2,1,0:T(2,128)(2,1)} %bitcast.25, bf16[256,256]{1,0:T(8,128)(2,1)S(1)} %reshape.59.other_ref, bf16[256,256]{1,0:T(8,128)(2,1)S(1)} %copy-done.3, bf16[256,256]{1,0:T(8,128)(2,1)S(1)} %dynamic-slice_bitcast_fusion.order_ref, ...), custom_call_target="tpu_custom_call" | custom-call | tf_op jit(solution)/shard_map/arrange/pallas_call | solution.py:608
  57.6 0.0 collective-permute-start.1
  57.6 0.1 iota_add_fusion
  57.7 7.3 %sort.7 = s32[32768]{0:T(1024)S(1)} sort(s32[32768]{0:T(1024)S(1)} %get-tuple-element.29), dimensions={0}, to_apply=%region_1.2 | sort | flops 491520 | bytes 262144 | tf_op jit(solution)/shard_map/sort | solution.py:556
  65.1 0.7 concatenate.7.point_ref
  65.7 5.6 %convert_reduce_fusion.first_ref = s32[259]{0:T(512)} fusion(s32[32768]{0:T(1024)S(1)} %get-tuple-element.30), kind=kLoop, calls=%fused_computation | loop fusion | flops 25460476 | bytes 132108 | tf_op jit(solution)/shard_map/reduce_sum | solution.py:558
  71.4 54.2 %collective-permute-done.1.joined_ref = bf16[16,512,128]{2,1,0:T(8,128)(2,1)} collective-permute-done((bf16[16,512,128]{2,1,0:T(8,128)(2,1)}, bf16[16,512,128]{2,1,0:T(8,128)(2,1)}, u32[]{:S(2)}, u32[]{:S(2)}) %collective-permute-start.1) | collective-permute-done | bytes 2097184 | tf_op jit(solution)/shard_map/ppermute | solution.py:656
  125.6 0.0 all-to-all-done.first_ref.second_ref.images_hbm
  125.6 6.5 %scores.1 = f32[8,128,128]{2,1,0:T(8,128)} custom-call(bf16[32,32,16,128]{3,2,1,0:T(8,128)(2,1)} %all-to-all-done.first_ref.second_ref.images_hbm, bf16[32,32,16,128]{3,2,1,0:T(8,128)(2,1)} %all-to-all-done.first_ref.second_ref.images_hbm, bf16[16,512,128]{2,1,0:T(8,128)(2,1)S(1)} %get-tuple-element.24.kept_ref, ...), custom_call_target="tpu_custom_call" | custom-call | tf_op jit(solution)/shard_map/scores/pallas_call | solution.py:187
  132.1 4.4 %all-to-all-start.1 = ((f32[8,128,128]{2,1,0:T(8,128)}), f32[8,128,128]{2,1,0:T(8,128)S(1)}, u32[]{:S(2)}, u32[]{:S(2)}) async-start(f32[8,128,128]{2,1,0:T(8,128)} %scores.1), calls=%async_computation.1 | async-start | bytes 1048576 | tf_op jit(solution)/shard_map/all_to_all | solution.py:689
  136.4 9.7 %all-to-all-done.1.parts_ref = f32[8,128,128]{2,1,0:T(8,128)S(1)} async-done(((f32[8,128,128]{2,1,0:T(8,128)}), f32[8,128,128]{2,1,0:T(8,128)S(1)}, u32[]{:S(2)}, u32[]{:S(2)}) %all-to-all-start.1) | async-done | bytes 524320 | tf_op jit(solution)/shard_map/all_to_all | solution.py:689
  146.2 0.8 copy-done.6
  147.0 66.7 %scatter.1 = (bf16[8,32,16,256]{3,2,1,0:T(8,128)(2,1)}, f32[2,2,256,16,128]{4,3,2,1,0:T(8,128)}) custom-call(s32[1]{0:T(128)} %bitcast.1.single_ref, s32[259]{0:T(512)} %convert_reduce_fusion.first_ref, s32[32896]{0:T(1024)} %concatenate.7.point_ref, f32[8,128,128]{2,1,0:T(8,128)} %copy-done.6, ...), custom_call_target="tpu_custom_call" | custom-call | tf_op jit(solution)/shard_map/scatter/pallas_call | solution.py:405
  213.7 3.6 %all-to-all-start.2 = ((bf16[8,32,16,256]{3,2,1,0:T(8,128)(2,1)}), bf16[8,32,16,256]{3,2,1,0:T(8,128)(2,1)S(1)}, u32[]{:S(2)}, u32[]{:S(2)}) async-start(bf16[8,32,16,256]{3,2,1,0:T(8,128)(2,1)} %get-tuple-element.27), calls=%async_computation.2 | async-start | bytes 4194304 | tf_op jit(solution)/shard_map/all_to_all | solution.py:696
  217.3 16.1 %planes.1 = bf16[8,32,16,256]{3,2,1,0:T(8,128)(2,1)} custom-call(f32[2,2,4096,128]{3,2,1,0:T(8,128)} %bitcast.23, bf16[768,256]{1,0:T(8,128)(2,1)} %constant.66.clone.y_ref, bf16[272,768]{1,0:T(8,128)(2,1)} %constant.67.clone.x_ref), custom_call_target="tpu_custom_call" | custom-call | tf_op jit(solution)/shard_map/planes/pallas_call | solution.py:504
  233.4 10.5 %all-to-all-done.2.refs_0_ = bf16[8,32,16,256]{3,2,1,0:T(8,128)(2,1)S(1)} async-done(((bf16[8,32,16,256]{3,2,1,0:T(8,128)(2,1)}), bf16[8,32,16,256]{3,2,1,0:T(8,128)(2,1)S(1)}, u32[]{:S(2)}, u32[]{:S(2)}) %all-to-all-start.2) | async-done | bytes 2097184 | tf_op jit(solution)/shard_map/all_to_all | solution.py:696
  243.9 4.4 %all-to-all-start.3 = ((bf16[8,32,16,256]{3,2,1,0:T(8,128)(2,1)}), bf16[8,32,16,256]{3,2,1,0:T(8,128)(2,1)}, u32[]{:S(2)}, u32[]{:S(2)}) async-start(bf16[8,32,16,256]{3,2,1,0:T(8,128)(2,1)} %planes.1), calls=%async_computation.3 | async-start | bytes 4194304 | tf_op jit(solution)/shard_map/all_to_all | solution.py:699
  248.2 26.6 %all-to-all-done.3.refs_1_ = bf16[8,32,16,256]{3,2,1,0:T(8,128)(2,1)} async-done(((bf16[8,32,16,256]{3,2,1,0:T(8,128)(2,1)}), bf16[8,32,16,256]{3,2,1,0:T(8,128)(2,1)}, u32[]{:S(2)}, u32[]{:S(2)}) %all-to-all-start.3) | async-done | bytes 2097184 | tf_op jit(solution)/shard_map/all_to_all | solution.py:699
  274.9 0.0 copy-done.4
  274.9 0.0 copy-done.5
  274.9 8.9 %volume.1 = f32[32,256,256]{2,1,0:T(8,128)} custom-call(s32[1]{0:T(128)} %bitcast.flip_ref, bf16[256,256]{1,0:T(8,128)(2,1)S(1)} %copy-done.5, bf16[512,256]{1,0:T(8,128)(2,1)S(1)} %copy-done.4, bf16[8,32,16,256]{3,2,1,0:T(8,128)(2,1)S(1)} %all-to-all-done.2.refs_0_, bf16[8,32,16,256]{3,2,1,0:T(8,128)(2,1)} %all-to-all-done.3.refs_1_), custom_call_target="tpu_custom_call" | custom-call | tf_op jit(solution)/shard_map/volume/pallas_call | solution.py:533
  (8 shorter events, 0.0 us)
Async XLA Ops:
  0.7 1.6 copy-start
  2.3 1.0 copy-start.1
  3.4 0.9 copy-start.2
  11.3 12.1 %slice-start = ((s32[128,4,256]{2,1,0:T(4,128)}), s32[128,1,256]{2,1,0:T(1,128)S(1)}, s32[]{:S(2)}) async-start(s32[128,4,256]{2,1,0:T(4,128)} %param.16), calls=%async_computation.4 | async-start | bytes 262144 | tf_op jit(solution)/shard_map/slice | solution.py:679
  11.3 12.2 %copy-start.7 = (f32[128,4,256]{2,1,0:T(4,128)S(1)}, f32[128,4,256]{2,1,0:T(4,128)}, u32[]{:S(2)}) copy-start(f32[128,4,256]{2,1,0:T(4,128)} %param.17) | copy-start | bytes 1572868
  11.3 114.2 %all-to-all-start = ((bf16[32,32,16,128]{3,2,1,0:T(8,128)(2,1)}), bf16[32,32,16,128]{3,2,1,0:T(8,128)(2,1)}, u32[]{:S(2)}, u32[]{:S(2)}) async-start(bf16[32,32,16,128]{3,2,1,0:T(8,128)(2,1)} %route.1), calls=%async_computation | async-start | bytes 8388608 | tf_op jit(solution)/shard_map/all_to_all | solution.py:676
  19.8 23.0 %collective-permute-start = (bf16[128,2,256]{2,1,0:T(2,128)(2,1)S(1)}, bf16[128,2,256]{2,1,0:T(2,128)(2,1)S(1)}, u32[]{:S(2)}, u32[]{:S(2)}) collective-permute-start(bf16[128,2,256]{2,1,0:T(2,128)(2,1)S(1)} %slice_bitcast_fusion), channel_id=1, source_target_pairs={{0,4},{1,0},{2,1},{3,2},{4,3},{8,12},{9,8},{10,9},{11,10},{12,11},... | collective-permute-start | bytes 393224 | tf_op jit(solution)/shard_map/ppermute | solution.py:652
  30.3 12.5 %copy-start.3 = (bf16[256,256]{1,0:T(8,128)(2,1)S(1)}, bf16[256,256]{1,0:T(8,128)(2,1)}, u32[]{:S(2)}) copy-start(bf16[256,256]{1,0:T(8,128)(2,1)} %constant.62.clone.eye_ref) | copy-start | bytes 393220
  57.6 67.9 %collective-permute-start.1 = (bf16[16,512,128]{2,1,0:T(8,128)(2,1)}, bf16[16,512,128]{2,1,0:T(8,128)(2,1)}, u32[]{:S(2)}, u32[]{:S(2)}) collective-permute-start(bf16[16,512,128]{2,1,0:T(8,128)(2,1)} %get-tuple-element.20), channel_id=1, source_target_pairs={{0,7},{1,6},{2,5},{3,4},{4,3},{5,2},{6,1},{7,0},{8,15},{9,14},{10,... | collective-permute-start | bytes 6291464 | tf_op jit(solution)/shard_map/ppermute | solution.py:656
  132.1 14.1 %all-to-all-start.1 = ((f32[8,128,128]{2,1,0:T(8,128)}), f32[8,128,128]{2,1,0:T(8,128)S(1)}, u32[]{:S(2)}, u32[]{:S(2)}) async-start(f32[8,128,128]{2,1,0:T(8,128)} %scores.1), calls=%async_computation.1 | async-start | bytes 1048576 | tf_op jit(solution)/shard_map/all_to_all | solution.py:689
  146.2 0.8 copy-start.6
  213.7 30.2 %all-to-all-start.2 = ((bf16[8,32,16,256]{3,2,1,0:T(8,128)(2,1)}), bf16[8,32,16,256]{3,2,1,0:T(8,128)(2,1)S(1)}, u32[]{:S(2)}, u32[]{:S(2)}) async-start(bf16[8,32,16,256]{3,2,1,0:T(8,128)(2,1)} %get-tuple-element.27), calls=%async_computation.2 | async-start | bytes 4194304 | tf_op jit(solution)/shard_map/all_to_all | solution.py:696
  233.4 41.5 %copy-start.4 = (bf16[512,256]{1,0:T(8,128)(2,1)S(1)}, bf16[512,256]{1,0:T(8,128)(2,1)}, u32[]{:S(2)}) copy-start(bf16[512,256]{1,0:T(8,128)(2,1)} %constant.69.clone.z_ref) | copy-start | bytes 786436
  233.4 41.5 %copy-start.5 = (bf16[256,256]{1,0:T(8,128)(2,1)S(1)}, bf16[256,256]{1,0:T(8,128)(2,1)}, u32[]{:S(2)}) copy-start(bf16[256,256]{1,0:T(8,128)(2,1)} %constant.68.clone.restore_ref) | copy-start | bytes 393220
  243.9 31.0 %all-to-all-start.3 = ((bf16[8,32,16,256]{3,2,1,0:T(8,128)(2,1)}), bf16[8,32,16,256]{3,2,1,0:T(8,128)(2,1)}, u32[]{:S(2)}, u32[]{:S(2)}) async-start(bf16[8,32,16,256]{3,2,1,0:T(8,128)(2,1)} %planes.1), calls=%async_computation.3 | async-start | bytes 4194304 | tf_op jit(solution)/shard_map/all_to_all | solution.py:699
where the time goes:
time: 286 us; the launch traced here: 284 us
  Pallas kernels  120 us (42%)
  waiting for transfers between devices  105 us (37%)
  starting transfers between devices  23.4 us (8%)
  local copies, waits for them, and re-layouts  21.8 us (8%)
  other arithmetic  13.4 us (5%)
    pallas_call x1, Pallas kernels, scatter_call(): pl.pallas_call(functools.partial(scatter_kernel, cap, width, grid, slabs)...  66.7 us
    ppermute x1, waiting for transfers between devices, paired_rows(): lax.ppermute(sent, 'vol', [(i, slabs - 1 - i) for i in range(slabs)])  54.2 us
    all_to_all x2, waiting for transfers between devices, shards(): lax.all_to_all(sent, 'vol', split_axis=0, concat_axis=0, tiled=True)  37.1 us
    pallas_call x1, Pallas kernels, planes_call(): pl.pallas_call(functools.partial(plane_kernel, slabs, grid), in_specs=[vm...  16.1 us
    pallas_call x1, Pallas kernels, arrange_call(): pl.pallas_call(arrange_kernel, out_shape=(shape, shape), in_specs=[vmem]...  14.8 us
    all_to_all x1, waiting for transfers between devices, shards(): lax.all_to_all(partial_value, 'vol', split_axis=0, concat_axis=0, tiled=T...  9.74 us
    pallas_call x1, Pallas kernels, volume_call(): pl.pallas_call(volume_kernel, grid_spec=pltpu.PrefetchScalarGridSpec(num_...  8.94 us
    all_to_all x2, starting transfers between devices, shards(): lax.all_to_all(sent, 'vol', split_axis=0, concat_axis=0, tiled=True)  7.97 us
  transfers between devices with their start and end apart: 6, of which 5 were waited for; matrix products, arithmetic and copies ran while one was open for 11% of the time, Pallas kernels for 11%

commit v1 on v0

--- a/solution.py
+++ b/solution.py
@@ -76,12 +76,6 @@
     return table_y, table_x, table_z, restore
 
 
-def lane_order(grid, slabs):
-    rows = plane_pairs(grid, slabs).transpose(0, 2, 1).reshape(-1)
-    source = (2 * rows[:, None] + np.arange(2)[None, :]).reshape(-1)
-    return (np.arange(2 * grid)[:, None] == source[None, :]).astype(jnp.bfloat16)
-
-
 def dot(a, b):
     return jnp.dot(a, b, preferred_element_type=F32)
 
@@ -96,8 +90,20 @@
     return high, low
 
 
-def route_kernel(cap, slabs, width, classes_ref, images_ref, eye_ref, order_ref, out_ref, lines):
+def route_kernel(cap, slabs, width, classes_ref, images_ref, out_ref, lines, eye_ref, order_ref):
     count, _, _, grid = images_ref.shape
+    eye = lax.broadcasted_iota(jnp.int32, (grid, grid), 0) == lax.broadcasted_iota(jnp.int32, (grid, grid), 1)
+    eye_ref[...] = eye.astype(F32).astype(BF16)
+    half = width // 4
+    bits = width.bit_length() - 1
+    value = lax.broadcasted_iota(jnp.int32, (8, 2 * grid), 1)
+    slab, pair = value >> bits, (value >> 1) & (half - 1)
+    first = 2 * half * slab + jnp.where(slab < slabs // 2, 1 + pair, half - 1 - pair)
+    both = jnp.where(2 * first == grid, 0, first)
+    row = jnp.where(value & (2 * half) == 0, both, jnp.where(2 * first == grid, first, grid - first))
+    source = (2 * row + (value & 1))[0:1, :]
+    order = lax.broadcasted_iota(jnp.int32, (2 * grid, 2 * grid), 0) == source
+    order_ref[...] = order.astype(F32).astype(BF16)
     halves = LANES // width
     piece = grid // halves
     lane = lax.broadcasted_iota(jnp.int32, (piece, LANES), 1)
@@ -125,19 +131,23 @@
     out_ref[...] = lines[...].astype(BF16).reshape(out_ref.shape)
 
 
-def route_call(images, assignment, eye, order, class_count, slabs, width, cap):
+def route_call(images, assignment, class_count, slabs, width, cap):
     count, grid = images.shape[0], images.shape[1]
     rows = grid // (LANES // width) * cap
     vmem = pl.BlockSpec(memory_space=VMEM)
     return pl.pallas_call(
         functools.partial(route_kernel, cap, slabs, width),
         out_shape=jax.ShapeDtypeStruct((class_count * slabs, rows // 16, 16, LANES), BF16),
-        in_specs=[pl.BlockSpec(memory_space=pltpu.SMEM)] + [vmem] * 3,
+        in_specs=[pl.BlockSpec(memory_space=pltpu.SMEM), vmem],
         out_specs=vmem,
-        scratch_shapes=[VMEM((class_count * slabs, rows, LANES), F32)],
+        scratch_shapes=[
+            VMEM((class_count * slabs, rows, LANES), F32),
+            VMEM((grid, grid), BF16),
+            VMEM((2 * grid, 2 * grid), BF16),
+        ],
         compiler_params=pltpu.CompilerParams(vmem_limit_bytes=48 * 2**20),
         name="route",
-    )(assignment, images, eye, order)
+    )(assignment, images)
 
 
 def score_kernel(cap, dirs, unit, first_ref, second_ref, kept_ref, joined_ref, out_ref, sums):
@@ -412,7 +422,7 @@
             VMEM((points, LANES), F32),
             VMEM((3 * width, grid), F32),
             VMEM((weights.shape[1], sources * rows16), BF16),
-            VMEM((sides, grid * step, LANES), F32),
+            VMEM((sides, grid, step + PAD, LANES), F32),
             VMEM(images.shape, BF16),
             VMEM(weights.shape, F32),
             pltpu.SemaphoreType.DMA,
@@ -433,6 +443,8 @@
     rows = half + 8
     slab = grid // slabs
     count = 2 * pairs
+    pitch = count + PAD
+    flat = lines.reshape(grid // LANES, grid * pitch, LANES)
     lane = lax.broadcasted_iota(jnp.int32, (grid, half), 1)
 
     def transformed(real, imag):
@@ -471,8 +483,8 @@
             for part in range(grid // LANES):
                 cut = slice(part * LANES, (part + 1) * LANES)
                 place = 2 * i + c
-                lines[part, pl.ds(place, half, stride=count), :] = plus[:half, cut]
-                lines[part, pl.ds(half * count + place, half, stride=count), :] = minus[1 : half + 1, cut]
+                flat[part, pl.ds(place, half, stride=pitch), :] = plus[:half, cut]
+                flat[part, pl.ds(half * pitch + place, half, stride=pitch), :] = minus[1 : half + 1, cut]
         return carry
 
     lax.fori_loop(0, pairs, one, 0, unroll=2)
@@ -481,10 +493,9 @@
             start = slab * d
         else:
             start = half + grid - slab * d - slab
-        size = slab * count
         for part in range(grid // LANES):
-            block = lines[part, start * count : start * count + size, :]
-            out_ref[d, :, :, part * LANES : (part + 1) * LANES] = block.astype(BF16).reshape(slab, count, LANES)
+            block = lines[part, start : start + slab, :count, :]
+            out_ref[d, :, :, part * LANES : (part + 1) * LANES] = block.astype(BF16)
 
 
 def plane_kernel(slabs, grid, data_ref, y_ref, x_ref, out_ref, lines):
@@ -505,7 +516,7 @@
         functools.partial(plane_kernel, slabs, grid),
         in_specs=[vmem] * 3,
         out_specs=vmem,
-        scratch_shapes=[VMEM((data.shape[0], grid * step, LANES), F32)],
+        scratch_shapes=[VMEM((data.shape[0], grid, step + PAD, LANES), F32)],
         out_shape=jax.ShapeDtypeStruct((slabs, slab, step, grid), BF16),
         compiler_params=pltpu.CompilerParams(vmem_limit_bytes=56 * 2**20),
         name="planes",
@@ -670,8 +681,7 @@
     groups = grid // (halves * steps)
 
     eye = jnp.asarray(np.eye(grid), BF16)
-    order = jnp.asarray(lane_order(grid, slab_count))
-    outgoing = route_call(images, assignment, eye, order, class_count, slab_count, width, capacity)
+    outgoing = route_call(images, assignment, class_count, slab_count, width, capacity)
     outgoing, projections = lax.optimization_barrier((outgoing, projections))
     arrived = lax.all_to_all(outgoing, ("cls", "vol"), split_axis=0, concat_axis=0, tiled=True)
 

time: 286 us -> 283 us (0.990)
  no operation moved by 1% of the time
where the time goes in v1:
time: 283 us; the launch traced here: 281 us
  Pallas kernels  118 us (42%)
  waiting for transfers between devices  106 us (37%)
  starting transfers between devices  23.4 us (8%)
  local copies, waits for them, and re-layouts  19.8 us (7%)
  other arithmetic  13.4 us (5%)
    pallas_call x1, Pallas kernels, scatter_call(): pl.pallas_call(functools.partial(scatter_kernel, cap, width, grid, slabs)...  65.6 us
    ppermute x1, waiting for transfers between devices, paired_rows(): lax.ppermute(sent, 'vol', [(i, slabs - 1 - i) for i in range(slabs)])  54.1 us
    all_to_all x2, waiting for transfers between devices, shards(): lax.all_to_all(sent, 'vol', split_axis=0, concat_axis=0, tiled=True)  38.2 us
    pallas_call x1, Pallas kernels, planes_call(): pl.pallas_call(functools.partial(plane_kernel, slabs, grid), in_specs=[vm...  15 us
    pallas_call x1, Pallas kernels, arrange_call(): pl.pallas_call(arrange_kernel, out_shape=(shape, shape), in_specs=[vmem]...  14.8 us
    all_to_all x1, waiting for transfers between devices, shards(): lax.all_to_all(partial_value, 'vol', split_axis=0, concat_axis=0, tiled=T...  9.74 us
    pallas_call x1, Pallas kernels, volume_call(): pl.pallas_call(volume_kernel, grid_spec=pltpu.PrefetchScalarGridSpec(num_...  8.94 us
    all_to_all x2, starting transfers between devices, shards(): lax.all_to_all(sent, 'vol', split_axis=0, concat_axis=0, tiled=True)  7.96 us
  transfers between devices with their start and end apart: 6, of which 5 were waited for; matrix products, arithmetic and copies ran while one was open for 11% of the time, Pallas kernels for 11%

profile of v1, /device:TPU:0, one launch (start us, length us, event | category | flops | bytes accessed | tf_op | source)
XLA Modules:
  0.0 280.9 jit_solution(756135163881239318)
XLA Ops:
  0.0 0.7 copy.22.classes_ref
  0.7 0.0 copy-start
  0.7 1.6 copy-done
  2.3 7.1 %route.1 = bf16[32,32,16,128]{3,2,1,0:T(8,128)(2,1)} custom-call(s32[8,1]{1,0:T(8,128)S(1)} %copy.22.classes_ref, bf16[8,256,2,256]{3,2,1,0:T(2,128)(2,1)S(1)} %copy-done), custom_call_target="tpu_custom_call" | custom-call | tf_op jit(solution)/shard_map/route/pallas_call | solution.py:138
  9.5 0.0 slice-start
  9.5 0.0 copy-start.5
  9.5 7.4 %all-to-all-start = ((bf16[32,32,16,128]{3,2,1,0:T(8,128)(2,1)}), bf16[32,32,16,128]{3,2,1,0:T(8,128)(2,1)}, u32[]{:S(2)}, u32[]{:S(2)}) async-start(bf16[32,32,16,128]{3,2,1,0:T(8,128)(2,1)} %route.1), calls=%async_computation | async-start | bytes 8388608 | tf_op jit(solution)/shard_map/all_to_all | solution.py:686
  16.9 1.0 slice_bitcast_fusion
  17.9 3.6 %collective-permute-start = (bf16[128,2,256]{2,1,0:T(2,128)(2,1)S(1)}, bf16[128,2,256]{2,1,0:T(2,128)(2,1)S(1)}, u32[]{:S(2)}, u32[]{:S(2)}) collective-permute-start(bf16[128,2,256]{2,1,0:T(2,128)(2,1)S(1)} %slice_bitcast_fusion), channel_id=1, source_target_pairs={{0,4},{1,0},{2,1},{3,2},{4,3},{8,12},{9,8},{10,9},{11,10},{12,11},... | collective-permute-start | bytes 393224 | tf_op jit(solution)/shard_map/ppermute | solution.py:663
  21.5 0.0 slice-done
  21.5 0.1 copy.30
  21.6 0.0 copy-done.5
  21.6 0.3 copy.24
  21.9 0.1 pad.8.clone
  22.0 0.1 and_convert_fusion
  22.1 0.2 maximum_maximum_fusion
  22.4 0.7 dynamic-slice_bitcast_fusion.1.extra_ref
  23.1 0.3 copy.25
  23.4 0.4 reshape.61
  23.8 4.6 %copy.26 = f32[32,512,16]{2,1,0:T(8,128)} copy(f32[32,512,16]{1,2,0:T(8,128)S(1)} %reshape.61) | data formatting | bytes 2097152 | tf_op jit(solution)/shard_map/reshape | solution.py:692
  28.4 0.0 copy-start.3
  28.4 7.6 %pad.5.weights_hbm = f32[32,512,128]{2,1,0:T(8,128)} pad(f32[32,512,16]{2,1,0:T(8,128)} %copy.26, f32[]{:T(128)} %constant.55.clone.1), padding=0_0x0_0x0_112 | pad | bytes 9437188 | tf_op jit(solution)/shard_map/jit(_pad)/pad | solution.py:693
  36.0 0.9 dynamic-slice_bitcast_fusion.order_ref
  36.9 3.9 %collective-permute-done = bf16[128,2,256]{2,1,0:T(2,128)(2,1)S(1)} collective-permute-done((bf16[128,2,256]{2,1,0:T(2,128)(2,1)S(1)}, bf16[128,2,256]{2,1,0:T(2,128)(2,1)S(1)}, u32[]{:S(2)}, u32[]{:S(2)}) %collective-permute-start) | collective-permute-done | bytes 131104 | tf_op jit(solution)/shard_map/ppermute | solution.py:663
  40.9 0.1 reshape.59.other_ref
  40.9 0.0 copy-done.3
  41.0 14.8 %arrange.1 = (bf16[16,512,128]{2,1,0:T(8,128)(2,1)S(1)}, bf16[16,512,128]{2,1,0:T(8,128)(2,1)}) custom-call(bf16[128,32,2,256]{3,2,1,0:T(2,128)(2,1)} %bitcast.25, bf16[256,256]{1,0:T(8,128)(2,1)S(1)} %reshape.59.other_ref, bf16[256,256]{1,0:T(8,128)(2,1)S(1)} %copy-done.3, bf16[256,256]{1,0:T(8,128)(2,1)S(1)} %dynamic-slice_bitcast_fusion.order_ref, ...), custom_call_target="tpu_custom_call" | custom-call | tf_op jit(solution)/shard_map/arrange/pallas_call | solution.py:619
  55.8 0.0 collective-permute-start.1
  55.8 0.1 iota_add_fusion
  55.9 7.3 %sort.7 = s32[32768]{0:T(1024)S(1)} sort(s32[32768]{0:T(1024)S(1)} %get-tuple-element.29), dimensions={0}, to_apply=%region_1.2 | sort | flops 491520 | bytes 262144 | tf_op jit(solution)/shard_map/sort | solution.py:567
  63.2 0.7 concatenate.7.point_ref
  63.9 5.7 %convert_reduce_fusion.first_ref = s32[259]{0:T(512)} fusion(s32[32768]{0:T(1024)S(1)} %get-tuple-element.30), kind=kLoop, calls=%fused_computation | loop fusion | flops 25460476 | bytes 132108 | tf_op jit(solution)/shard_map/reduce_sum | solution.py:569
  69.5 54.1 %collective-permute-done.1.joined_ref = bf16[16,512,128]{2,1,0:T(8,128)(2,1)} collective-permute-done((bf16[16,512,128]{2,1,0:T(8,128)(2,1)}, bf16[16,512,128]{2,1,0:T(8,128)(2,1)}, u32[]{:S(2)}, u32[]{:S(2)}) %collective-permute-start.1) | collective-permute-done | bytes 2097184 | tf_op jit(solution)/shard_map/ppermute | solution.py:667
  123.7 0.0 all-to-all-done.first_ref.second_ref.images_hbm
  123.7 6.5 %scores.1 = f32[8,128,128]{2,1,0:T(8,128)} custom-call(bf16[32,32,16,128]{3,2,1,0:T(8,128)(2,1)} %all-to-all-done.first_ref.second_ref.images_hbm, bf16[32,32,16,128]{3,2,1,0:T(8,128)(2,1)} %all-to-all-done.first_ref.second_ref.images_hbm, bf16[16,512,128]{2,1,0:T(8,128)(2,1)S(1)} %get-tuple-element.24.kept_ref, ...), custom_call_target="tpu_custom_call" | custom-call | tf_op jit(solution)/shard_map/scores/pallas_call | solution.py:197
  130.2 4.4 %all-to-all-start.1 = ((f32[8,128,128]{2,1,0:T(8,128)}), f32[8,128,128]{2,1,0:T(8,128)S(1)}, u32[]{:S(2)}, u32[]{:S(2)}) async-start(f32[8,128,128]{2,1,0:T(8,128)} %scores.1), calls=%async_computation.1 | async-start | bytes 1048576 | tf_op jit(solution)/shard_map/all_to_all | solution.py:699
  134.6 9.7 %all-to-all-done.1.parts_ref = f32[8,128,128]{2,1,0:T(8,128)S(1)} async-done(((f32[8,128,128]{2,1,0:T(8,128)}), f32[8,128,128]{2,1,0:T(8,128)S(1)}, u32[]{:S(2)}, u32[]{:S(2)}) %all-to-all-start.1) | async-done | bytes 524320 | tf_op jit(solution)/shard_map/all_to_all | solution.py:699
  144.3 0.0 copy-start.4
  144.3 0.8 copy-done.4
  145.1 65.6 %scatter.1 = (bf16[8,32,16,256]{3,2,1,0:T(8,128)(2,1)}, f32[2,2,256,16,128]{4,3,2,1,0:T(8,128)}) custom-call(s32[1]{0:T(128)} %bitcast.1.single_ref, s32[259]{0:T(512)} %convert_reduce_fusion.first_ref, s32[32896]{0:T(1024)} %concatenate.7.point_ref, f32[8,128,128]{2,1,0:T(8,128)} %copy-done.4, ...), custom_call_target="tpu_custom_call" | custom-call | tf_op jit(solution)/shard_map/scatter/pallas_call | solution.py:415
  210.7 3.6 %all-to-all-start.2 = ((bf16[8,32,16,256]{3,2,1,0:T(8,128)(2,1)}), bf16[8,32,16,256]{3,2,1,0:T(8,128)(2,1)S(1)}, u32[]{:S(2)}, u32[]{:S(2)}) async-start(bf16[8,32,16,256]{3,2,1,0:T(8,128)(2,1)} %get-tuple-element.27), calls=%async_computation.2 | async-start | bytes 4194304 | tf_op jit(solution)/shard_map/all_to_all | solution.py:706
  214.4 15.0 %planes.1 = bf16[8,32,16,256]{3,2,1,0:T(8,128)(2,1)} custom-call(f32[2,2,4096,128]{3,2,1,0:T(8,128)} %bitcast.23, bf16[768,256]{1,0:T(8,128)(2,1)} %constant.63.clone.y_ref, bf16[272,768]{1,0:T(8,128)(2,1)} %constant.64.clone.x_ref), custom_call_target="tpu_custom_call" | custom-call | tf_op jit(solution)/shard_map/planes/pallas_call | solution.py:515
  229.4 11.5 %all-to-all-done.2.refs_0_ = bf16[8,32,16,256]{3,2,1,0:T(8,128)(2,1)S(1)} async-done(((bf16[8,32,16,256]{3,2,1,0:T(8,128)(2,1)}), bf16[8,32,16,256]{3,2,1,0:T(8,128)(2,1)S(1)}, u32[]{:S(2)}, u32[]{:S(2)}) %all-to-all-start.2) | async-done | bytes 2097184 | tf_op jit(solution)/shard_map/all_to_all | solution.py:706
  240.9 4.3 %all-to-all-start.3 = ((bf16[8,32,16,256]{3,2,1,0:T(8,128)(2,1)}), bf16[8,32,16,256]{3,2,1,0:T(8,128)(2,1)}, u32[]{:S(2)}, u32[]{:S(2)}) async-start(bf16[8,32,16,256]{3,2,1,0:T(8,128)(2,1)} %planes.1), calls=%async_computation.3 | async-start | bytes 4194304 | tf_op jit(solution)/shard_map/all_to_all | solution.py:709
  245.3 26.6 %all-to-all-done.3.refs_1_ = bf16[8,32,16,256]{3,2,1,0:T(8,128)(2,1)} async-done(((bf16[8,32,16,256]{3,2,1,0:T(8,128)(2,1)}), bf16[8,32,16,256]{3,2,1,0:T(8,128)(2,1)}, u32[]{:S(2)}, u32[]{:S(2)}) %all-to-all-start.3) | async-done | bytes 2097184 | tf_op jit(solution)/shard_map/all_to_all | solution.py:709
  271.9 0.0 copy-done.1
  271.9 0.0 copy-done.2
  271.9 8.9 %volume.1 = f32[32,256,256]{2,1,0:T(8,128)} custom-call(s32[1]{0:T(128)} %bitcast.flip_ref, bf16[256,256]{1,0:T(8,128)(2,1)S(1)} %copy-done.2, bf16[512,256]{1,0:T(8,128)(2,1)S(1)} %copy-done.1, bf16[8,32,16,256]{3,2,1,0:T(8,128)(2,1)S(1)} %all-to-all-done.2.refs_0_, bf16[8,32,16,256]{3,2,1,0:T(8,128)(2,1)} %all-to-all-done.3.refs_1_), custom_call_target="tpu_custom_call" | custom-call | tf_op jit(solution)/shard_map/volume/pallas_call | solution.py:544
  (4 shorter events, 0.0 us)
Async XLA Ops:
  0.7 1.6 copy-start
  9.5 12.1 %slice-start = ((s32[128,4,256]{2,1,0:T(4,128)}), s32[128,1,256]{2,1,0:T(1,128)S(1)}, s32[]{:S(2)}) async-start(s32[128,4,256]{2,1,0:T(4,128)} %param.15), calls=%async_computation.4 | async-start | bytes 262144 | tf_op jit(solution)/shard_map/slice | solution.py:689
  9.5 12.2 %copy-start.5 = (f32[128,4,256]{2,1,0:T(4,128)S(1)}, f32[128,4,256]{2,1,0:T(4,128)}, u32[]{:S(2)}) copy-start(f32[128,4,256]{2,1,0:T(4,128)} %param.16) | copy-start | bytes 1572868
  9.5 114.2 %all-to-all-start = ((bf16[32,32,16,128]{3,2,1,0:T(8,128)(2,1)}), bf16[32,32,16,128]{3,2,1,0:T(8,128)(2,1)}, u32[]{:S(2)}, u32[]{:S(2)}) async-start(bf16[32,32,16,128]{3,2,1,0:T(8,128)(2,1)} %route.1), calls=%async_computation | async-start | bytes 8388608 | tf_op jit(solution)/shard_map/all_to_all | solution.py:686
  17.9 23.0 %collective-permute-start = (bf16[128,2,256]{2,1,0:T(2,128)(2,1)S(1)}, bf16[128,2,256]{2,1,0:T(2,128)(2,1)S(1)}, u32[]{:S(2)}, u32[]{:S(2)}) collective-permute-start(bf16[128,2,256]{2,1,0:T(2,128)(2,1)S(1)} %slice_bitcast_fusion), channel_id=1, source_target_pairs={{0,4},{1,0},{2,1},{3,2},{4,3},{8,12},{9,8},{10,9},{11,10},{12,11},... | collective-permute-start | bytes 393224 | tf_op jit(solution)/shard_map/ppermute | solution.py:663
  28.4 12.5 %copy-start.3 = (bf16[256,256]{1,0:T(8,128)(2,1)S(1)}, bf16[256,256]{1,0:T(8,128)(2,1)}, u32[]{:S(2)}) copy-start(bf16[256,256]{1,0:T(8,128)(2,1)} %constant.60.clone.eye_ref) | copy-start | bytes 393220
  55.8 67.9 %collective-permute-start.1 = (bf16[16,512,128]{2,1,0:T(8,128)(2,1)}, bf16[16,512,128]{2,1,0:T(8,128)(2,1)}, u32[]{:S(2)}, u32[]{:S(2)}) collective-permute-start(bf16[16,512,128]{2,1,0:T(8,128)(2,1)} %get-tuple-element.20), channel_id=1, source_target_pairs={{0,7},{1,6},{2,5},{3,4},{4,3},{5,2},{6,1},{7,0},{8,15},{9,14},{10,... | collective-permute-start | bytes 6291464 | tf_op jit(solution)/shard_map/ppermute | solution.py:667
  130.2 14.1 %all-to-all-start.1 = ((f32[8,128,128]{2,1,0:T(8,128)}), f32[8,128,128]{2,1,0:T(8,128)S(1)}, u32[]{:S(2)}, u32[]{:S(2)}) async-start(f32[8,128,128]{2,1,0:T(8,128)} %scores.1), calls=%async_computation.1 | async-start | bytes 1048576 | tf_op jit(solution)/shard_map/all_to_all | solution.py:699
  144.3 0.8 copy-start.4
  210.7 30.2 %all-to-all-start.2 = ((bf16[8,32,16,256]{3,2,1,0:T(8,128)(2,1)}), bf16[8,32,16,256]{3,2,1,0:T(8,128)(2,1)S(1)}, u32[]{:S(2)}, u32[]{:S(2)}) async-start(bf16[8,32,16,256]{3,2,1,0:T(8,128)(2,1)} %get-tuple-element.27), calls=%async_computation.2 | async-start | bytes 4194304 | tf_op jit(solution)/shard_map/all_to_all | solution.py:706
  229.4 42.6 %copy-start.1 = (bf16[512,256]{1,0:T(8,128)(2,1)S(1)}, bf16[512,256]{1,0:T(8,128)(2,1)}, u32[]{:S(2)}) copy-start(bf16[512,256]{1,0:T(8,128)(2,1)} %constant.66.clone.z_ref) | copy-start | bytes 786436
  229.4 42.6 %copy-start.2 = (bf16[256,256]{1,0:T(8,128)(2,1)S(1)}, bf16[256,256]{1,0:T(8,128)(2,1)}, u32[]{:S(2)}) copy-start(bf16[256,256]{1,0:T(8,128)(2,1)} %constant.65.clone.restore_ref) | copy-start | bytes 393220
  240.9 31.0 %all-to-all-start.3 = ((bf16[8,32,16,256]{3,2,1,0:T(8,128)(2,1)}), bf16[8,32,16,256]{3,2,1,0:T(8,128)(2,1)}, u32[]{:S(2)}, u32[]{:S(2)}) async-start(bf16[8,32,16,256]{3,2,1,0:T(8,128)(2,1)} %planes.1), calls=%async_computation.3 | async-start | bytes 4194304 | tf_op jit(solution)/shard_map/all_to_all | solution.py:709
